TPU v7x, 128 devices: a whole 4x4x4 slice. The times are simulated.
128 devices in a mesh: dp: 8 (over y_lo, z), ctx: 16 (over x, y_hi, core).
Axes of the slice: x: 4, y: 4 (y_hi: 2, y_lo: 2; y = y_hi * 2 + y_lo), z: 4, core: 2. Of those that a mesh axis runs over, the one named last changes fastest.
Arguments:
- query_rows: bfloat16 [16, 4096, 2048], P('dp', 'ctx'), may hold values from -6 to 6
- key_rows: bfloat16 [16, 4096, 2048], P('dp', 'ctx'), may hold values from -6 to 6
- value_rows: bfloat16 [16, 4096, 2048], P('dp', 'ctx'), may hold values from -6 to 6
- out_grad: bfloat16 [16, 4096, 2048], P('dp', 'ctx'), may hold values from -6 to 6
- norm_gain: float32 [16, 128], replicated, may hold values from 0.1 to 1.9
- out_weight: bfloat16 [2048, 2048], P(('dp', 'ctx')), may hold values from -0.125 to 0.125
- start_block: int32 [16, 3], P('dp'), may hold values from 0 to 15, as said below
- start_offset: int32 [16, 3], P('dp'), may hold values from 0 to 255
Outputs:
- layer_out: bfloat16 [16, 4096, 2048], P('dp', 'ctx')
- query_grad: bfloat16 [16, 4096, 2048], P('dp', 'ctx')
- key_grad: bfloat16 [16, 4096, 2048], P('dp', 'ctx')
- value_grad: bfloat16 [16, 4096, 2048], P('dp', 'ctx')
- weight_grad: float32 [2048, 2048], P(('dp', 'ctx'))
Inputs may be any that keep to these rules, and one draw needn't show every extreme that they name: Position start_block * 256 + start_offset begins a document; the list of a sequence is unordered and may repeat.
All inputs are finite; a program needn't handle non-finite values.
Results may differ from a plain program's by a relative error of at most 0.0053.
Values may be sent and summed in bfloat16 or wider, within the bound.
A program may use at most 192 MiB of HBM per device.

v0:
```python
import math

import jax
import jax.numpy as jnp
from jax import lax
from jax.sharding import PartitionSpec as P

exact = lax.Precision.HIGHEST
epsilon = 1.0


def entering(value, axis, combine, identity, reverse):
    peers, here = (lax.axis_size(axis), lax.axis_index(axis))
    everything = jax.tree.map(lambda part: lax.all_gather(part, axis), value)
    start = jax.tree.map(
        lambda part, zero: jnp.broadcast_to(jnp.asarray(zero, part.dtype), part.shape),
        value,
        identity,
    )

    def hop(k, before):
        at = peers - 1 - k if reverse else k
        reached = at > here if reverse else at < here
        new = combine(before, jax.tree.map(lambda part: part[at], everything))
        return jax.tree.map(lambda a, b: jnp.where(reached, a, b), new, before)

    return lax.fori_loop(0, peers, hop, start)


def chain_join(earlier, later):
    keeping = 1.0 - later[1]
    return (later[0] + keeping[:, None, None, None] * earlier[0], jnp.maximum(earlier[1], later[1]))


def per_device(
    query_rows, key_rows, value_rows, out_grad, norm_gain, out_weight, start_block, start_offset
):
    seq_dp, block_len, width_hd = query_rows.shape
    heads, head_dim = norm_gain.shape
    width_out = out_grad.shape[2]
    dev_index = lax.axis_index("ctx")
    places = jnp.arange(block_len, dtype=jnp.int32)
    matched = (start_block[:, None, :] == dev_index) & (
        start_offset[:, None, :] == places[None, :, None]
    )
    local_doc = jnp.cumsum(jnp.any(matched, axis=2).astype(jnp.int32), axis=1)
    pre_start = (local_doc == 0).astype(jnp.float32)[:, :, None, None]
    end_mask = (local_doc == local_doc[:, -1:]).astype(jnp.float32)[:, :, None, None]
    reset_flag = (local_doc[:, -1] > 0).astype(jnp.float32)
    causal = (places[None, :, None] >= places[None, None, :]) & (
        local_doc[:, :, None] == local_doc[:, None, :]
    )
    causal_mask = causal.astype(jnp.float32)[:, None, :, :]
    shape4 = (seq_dp, block_len, heads, head_dim)
    query4 = query_rows.reshape(shape4)
    key4 = key_rows.reshape(shape4)
    value4 = value_rows.reshape(shape4)
    scores = (
        jnp.einsum("sthd,suhd->shtu", query4, key4, preferred_element_type=jnp.float32)
        * causal_mask
    ).astype(jnp.bfloat16)
    local_state = jnp.einsum(
        "sthd,sthe->shde",
        key4 * end_mask.astype(jnp.bfloat16),
        value4,
        preferred_element_type=jnp.float32,
    )
    zero_state = jnp.zeros_like(local_state)
    zero_flag = jnp.zeros_like(reset_flag)
    incoming = entering(
        (local_state, reset_flag), "ctx", chain_join, (zero_state, zero_flag), False
    )[0]
    att_out = jnp.einsum("shtu,suhd->sthd", scores, value4, preferred_element_type=jnp.float32)
    att_out = att_out + pre_start * jnp.einsum(
        "sthd,shde->sthe", query4.astype(jnp.float32), incoming, precision=exact
    )
    inv_rms = lax.rsqrt(jnp.mean(att_out * att_out, axis=3, keepdims=True) + epsilon)
    normed = (att_out * inv_rms * norm_gain).astype(jnp.bfloat16)
    flat_normed = normed.reshape(seq_dp * block_len, width_hd)
    flat_grad = out_grad.reshape(seq_dp * block_len, width_out)
    contract_cols = (((1,), (1,)), ((), ()))
    whole_weight = lax.all_gather(out_weight, ("dp", "ctx"), axis=0, tiled=True)
    layer_total = jnp.dot(flat_normed, whole_weight, preferred_element_type=jnp.float32)
    normed_grad = lax.dot_general(
        flat_grad, whole_weight, contract_cols, preferred_element_type=jnp.float32
    )
    layer_out = layer_total.astype(jnp.bfloat16).reshape(seq_dp, block_len, width_out)
    scaled = normed_grad.reshape(shape4) * norm_gain
    att_grad = inv_rms * (
        scaled - att_out * inv_rms * inv_rms * jnp.mean(scaled * att_out, axis=3, keepdims=True)
    )
    att_grad = att_grad.astype(jnp.bfloat16)
    back_state = jnp.einsum(
        "sthd,sthe->shde",
        query4 * pre_start.astype(jnp.bfloat16),
        att_grad,
        preferred_element_type=jnp.float32,
    )
    outgoing = entering((back_state, reset_flag), "ctx", chain_join, (zero_state, zero_flag), True)[
        0
    ]
    grad_scores = (
        jnp.einsum("sthd,suhd->shtu", att_grad, value4, preferred_element_type=jnp.float32)
        * causal_mask
    ).astype(jnp.bfloat16)
    query_grad = jnp.einsum(
        "shtu,suhd->sthd", grad_scores, key4, preferred_element_type=jnp.float32
    )
    query_grad = query_grad + pre_start * jnp.einsum(
        "sthb,shab->stha", att_grad.astype(jnp.float32), incoming, precision=exact
    )
    key_grad = jnp.einsum(
        "shtu,sthd->suhd", grad_scores, query4, preferred_element_type=jnp.float32
    )
    key_grad = key_grad + end_mask * jnp.einsum(
        "suhb,shab->suha", value4.astype(jnp.float32), outgoing, precision=exact
    )
    value_grad = jnp.einsum("shtu,sthd->suhd", scores, att_grad, preferred_element_type=jnp.float32)
    value_grad = value_grad + end_mask * jnp.einsum(
        "suha,shab->suhb", key4.astype(jnp.float32), outgoing, precision=exact
    )
    flat_shape = (seq_dp, block_len, width_hd)
    total_tokens = seq_dp * block_len * lax.axis_size("dp") * lax.axis_size("ctx")
    grad_scale = 1.0 / math.sqrt(total_tokens)
    contract_rows = (((0,), (0,)), ((), ()))
    weight_sum = lax.psum_scatter(
        lax.dot_general(flat_normed, flat_grad, contract_rows, preferred_element_type=jnp.float32),
        ("dp", "ctx"),
        scatter_dimension=0,
        tiled=True,
    )
    weight_grad = weight_sum * grad_scale
    return (
        layer_out,
        query_grad.reshape(flat_shape).astype(jnp.bfloat16),
        key_grad.reshape(flat_shape).astype(jnp.bfloat16),
        value_grad.reshape(flat_shape).astype(jnp.bfloat16),
        weight_grad,
    )


def solution(mesh):
    in_specs = (
        P("dp", "ctx", None),
        P("dp", "ctx", None),
        P("dp", "ctx", None),
        P("dp", "ctx", None),
        P(),
        P(("dp", "ctx"), None),
        P("dp", None),
        P("dp", None),
    )
    out_specs = (
        P("dp", "ctx", None),
        P("dp", "ctx", None),
        P("dp", "ctx", None),
        P("dp", "ctx", None),
        P(("dp", "ctx"), None),
    )
    return jax.shard_map(
        per_device, mesh=mesh, in_specs=in_specs, out_specs=out_specs, check_vma=False
    )
```

profile of v0, /device:TPU:1, one launch (start us, length us, event | category | flops | bytes accessed | tf_op | source)
XLA Modules:
  0.0 1419.4 jit_solution(17197948511837471187)
XLA Ops:
  14.3 4.3 copy.82
  18.6 4.2 fusion.12
  24.8 34.3 %all-reduce = f32[32]{0:T(128)S(1)} all-reduce(f32[32]{0:T(128)S(1)} %fusion.34), channel_id=3, replica_groups=mesh['dp'=8,'ctx'=16] {'ctx'}, use_global_device_ids=true, to_apply=%add | all-reduce | flops 32 | bytes 256
  72.6 143.0 %all-gather.7.cloned.1.call-done = bf16[2048,2048]{1,0:T(8,128)(2,1)} async-done(((bf16[16,2048]{1,0:T(8,128)(2,1)}), bf16[2048,2048]{1,0:T(8,128)(2,1)}) %all-gather.7.cloned.1.call-update) | async-done | bytes 8388624 | tf_op jit(solution)/shard_map/all_gather | solution.py:82
  215.6 9.5 fusion.16
  225.1 180.4 %all-gather.9.cloned.1.call-done = f32[32,16,128,128]{3,2,1,0:T(8,128)} async-done(((f32[2,16,128,128]{3,2,1,0:T(8,128)}), f32[32,16,128,128]{3,2,1,0:T(8,128)}) %all-gather.9.cloned.1.call-update) | async-done | bytes 33554448 | tf_op jit(solution)/shard_map/all_gather | solution.py:14
  405.4 65.1 %while.30 = (s32[]{:T(128)}, f32[2,16,128,128]{3,2,1,0:T(8,128)}, s32[]{:T(128)}, f32[16,2,16,128,128]{4,3,2,1,0:T(8,128)}, f32[16,2]{1,0:T(8,128)S(1)}, /*index=5*/s32[]{:T(128)}, s32[]{:T(128)}) while((s32[]{:T(128)}, f32[2,16,128,128]{3,2,1,0:T(8,128)}, s32[]{:T(128)}, f32[16,2,16,128,128]{4,3,2,1,0:T(8,128)}, ...), condition=%wide.region_4.5_spmd.clone, body=%wide.region_3.4_spmd.clone.sunk | while | flops 2097158 | bytes 6291593 | solution.py:27
  408.9 4.1 fusion.66
  413.0 4.1 fusion.66
  417.1 4.1 fusion.66
  421.2 4.1 fusion.66
  425.3 4.1 fusion.66
  429.4 4.1 fusion.66
  433.5 4.1 fusion.66
  437.7 4.1 fusion.66
  441.8 4.1 fusion.66
  445.9 4.1 fusion.66
  450.0 4.1 fusion.66
  454.1 4.1 fusion.66
  458.2 4.1 fusion.66
  462.3 4.1 fusion.66
  470.5 8.0 multiply_reduce_fusion
  481.3 4.5 copy.86
  485.9 9.9 fusion.4
  511.8 4.1 copy.97
  515.9 5.0 fusion.38
  520.9 9.3 convolution_convert_fusion
  530.1 626.4 %reduce-scatter.2.cloned.1.call-done = f32[16,2048]{1,0:T(8,128)} async-done(((f32[2048,2048]{1,0:T(8,128)}), f32[16,2048]{1,0:T(8,128)}) %reduce-scatter.2.cloned.1.call-update) | async-done | bytes 131088 | tf_op jit(solution)/shard_map/reduce_scatter | solution.py:126
  1158.1 189.4 %all-gather.11.cloned.1.call-done = f32[32,16,128,128]{3,2,1,0:T(8,128)} async-done(((f32[2,16,128,128]{3,2,1,0:T(8,128)}), f32[32,16,128,128]{3,2,1,0:T(8,128)}) %all-gather.11.cloned.1.call-update) | async-done | bytes 33554448 | tf_op jit(solution)/shard_map/all_gather | solution.py:14
  1347.4 42.3 %while.31 = (s32[]{:T(128)}, f32[2,16,128,128]{3,2,1,0:T(8,128)S(1)}, s32[]{:T(128)}, f32[16,2,16,128,128]{4,3,2,1,0:T(8,128)}, f32[16,2]{1,0:T(8,128)S(1)}, /*index=5*/s32[]{:T(128)}, s32[]{:T(128)}, s32[]{:T(128)}, s32[]{:T(128)}) while((s32[]{:T(128)}, f32[2,16,128,128]{3,2,1,0:T(8,128)S(1)}, s32[]{:T(128)}, ...), condition=%wide.region_8.9_spmd.clone, body=%wide.region_7.8_spmd.clone.sunk | while | flops 2097162 | bytes 6291655 | solution.py:27
  1389.8 5.6 fusion.9
  1403.2 5.7 fusion.2
  (128 shorter events, 103.4 us)
Async XLA Ops:
  7.2 208.4 %copy-start = (bf16[2,256,2048]{2,1,0:T(8,128)(2,1)S(1)}, bf16[2,256,2048]{2,1,0:T(8,128)(2,1)}, u32[]{:S(2)}) copy-start(bf16[2,256,2048]{2,1,0:T(8,128)(2,1)} %param.15) | copy-start | bytes 6291460
  7.2 208.4 %all-gather.7.cloned.1.call-start = ((), (), s32[]{:S(2)}) async-start(), calls=%async_computation.1 | async-start | bytes 8454144 | tf_op jit(solution)/shard_map/all_gather | solution.py:82
  7.9 397.5 %all-gather.9.cloned.1.call-start = ((), (), s32[]{:S(2)}) async-start(), calls=%async_computation.3 | async-start | bytes 35651584 | tf_op jit(solution)/shard_map/all_gather | solution.py:14
  22.8 0.7 copy-start.17
  22.9 1133.6 %reduce-scatter.2.cloned.1.call-start = ((), (), s32[]{:S(2)}) async-start(), calls=%async_computation.2 | async-start | bytes 16908288 | tf_op jit(solution)/shard_map/reduce_scatter | solution.py:126
  63.4 5.7 copy-start.10
  67.1 2.0 copy-start.8
  405.4 65.1 %copy-start.16 = (f32[16,128]{1,0:T(8,128)S(1)}, f32[16,128]{1,0:T(8,128)}, u32[]{:S(2)}) copy-start(f32[16,128]{1,0:T(8,128)} %param.16) | copy-start | bytes 24580
  470.5 8.0 copy-start.14
  495.7 1.6 copy-start.4
  495.7 851.7 %all-gather.11.cloned.1.call-start = ((), (), s32[]{:S(2)}) async-start(), calls=%async_computation.4 | async-start | bytes 35651584 | tf_op jit(solution)/shard_map/all_gather | solution.py:14
  501.0 3.1 copy-start.11
  504.1 2.1 copy-start.9
  504.1 3.1 copy-start.2
  504.1 3.8 copy-start.5
  511.8 4.1 copy-start.6
  515.9 5.0 copy-start.15
  520.9 826.6 %copy-start.3 = (f32[2,16,128,128]{3,2,1,0:T(8,128)S(1)}, f32[2,16,128,128]{3,2,1,0:T(8,128)}, u32[]{:S(2)}) copy-start(f32[2,16,128,128]{3,2,1,0:T(8,128)} %custom-call.1) | copy-start | bytes 6291460
  1389.8 5.6 copy-start.12
  1389.8 5.6 copy-start.13
  1399.1 4.1 copy-start.7
  1408.8 4.1 copy-start.1
Sparse Core Ops, SparseCore 0:
  9.7 205.7 all-gather.6
  218.5 186.8 all-gather.8
  495.9 660.5 reduce-scatter.1
  1158.7 188.6 all-gather.10
where the time goes:
time: 1420 us
  waiting for transfers between devices  1140 us (80%)
  other arithmetic  114 us (8%)
  matrix products  80 us (6%)
  local copies, waits for them, and re-layouts  36 us (3%)
  blocking collectives  34.3 us (2%)
  between operations  14.6 us (1%)
    reduce_scatter x1, waiting for transfers between devices, per_device(): lax.psum_scatter(lax.dot_general(flat_normed, flat_grad, contract_rows, p...  626 us
    all_gather x2, waiting for transfers between devices, entering(): everything = jax.tree.map(lambda part: lax.all_gather(part, axis), value)  370 us
    all_gather x1, waiting for transfers between devices, per_device(): whole_weight = lax.all_gather(out_weight, ('dp', 'ctx'), axis=0, tiled=True)  143 us
    select_n x32, other arithmetic, hop(): return jax.tree.map(lambda a, b: jnp.where(reached, a, b), new, before)  106 us
    unnamed x1, blocking collectives  34.3 us
  transfers between devices with their start and end apart: 4, of which 4 were waited for; matrix products, arithmetic and copies ran while one was open for 5% of the time, Pallas kernels for 0%

commit v1 on v0

v1 whole, which is shorter than its diff:
```python
import functools
import math

import jax
import jax.numpy as jnp
from jax import lax
from jax.experimental import pallas as pl
from jax.experimental.pallas import tpu as pltpu
from jax.sharding import PartitionSpec as P

BF, F32 = jnp.bfloat16, jnp.float32
MESH = pl.DeviceIdType.MESH
T, H, D, W = 256, 16, 128, 2048
HALF = W // 2
PIECES = ((0, 384, "yxz"), (384, 384, "zyx"), (768, 256, "xzy"))
NT = (((1,), (1,)), ((), ()))
TN = (((0,), (0,)), ((), ()))
NN = (((1,), (0,)), ((), ()))


def dot(a, b, dims):
    return lax.dot_general(a, b, dims, preferred_element_type=F32)


def where_am_i():
    dp, ctx = lax.axis_index("dp"), lax.axis_index("ctx")
    return (ctx // 4, 2 * ((ctx // 2) % 2) + dp // 4, dp % 4, ctx % 2)


def device(at):
    x, y, z, c = at
    return ((y % 2) * 4 + z, (x * 2 + y // 2) * 2 + c)


def moved(at, axis, k):
    x, y, z, c = at
    if axis == "x":
        return ((x + k) % 4, y, z, c)
    if axis == "y":
        return (x, (y + k) % 4, z, c)
    if axis == "z":
        return (x, y, (z + k) % 4, c)
    return (x, y, z, 1 - c)


def chips(ref, at, held, free, cols=None, lead=()):
    x, y, z, _ = at
    every = slice(None)
    parts = (("y", y % 2), ("z", z), ("x", x), ("y", y // 2))
    index = tuple(every if axis in free else place for axis, place in parts if axis in held)
    tail = (every,) if cols is None else (every, cols)
    return ref.at[tuple(lead) + index + tail]


def set_dims(held):
    return tuple(n for axis, n in (("y", 2), ("z", 4), ("x", 4), ("y", 2)) if axis in held)


def remote(src, dst, ssem, rsem, at):
    return pltpu.make_async_remote_copy(
        src_ref=src, dst_ref=dst, send_sem=ssem, recv_sem=rsem, device_id=device(at), device_id_type=MESH
    )


class Scan:
    HOPS = tuple((dx, dh) for dx in range(4) for dh in range(2) if dx or dh)

    def __init__(self, me, backward, fresh, other, tot, arr, car, back, mine, result, send, recv, sb):
        self.me, self.backward = me, backward
        self.fresh, self.other, self.tot, self.arr = fresh, other, tot, arr
        self.car, self.back, self.mine, self.result = car, back, mine, result
        self.send, self.recv, self.sb = send, recv, sb
        x, y, _, c = me
        self.c, self.g = c, x * 2 + y // 2
        self.sib = moved(me, "c", 1)
        self.block = self.g * 2 + c
        self.sib_block = self.g * 2 + 1 - c
        self.second = (c == 0) if backward else (c == 1)

    def keep(self, test):
        hit = test(self.sb[self.c, 0]) | test(self.sb[self.c, 1]) | test(self.sb[self.c, 2])
        return jnp.where(hit, 0.0, 1.0).astype(F32)

    def other_copy(self):
        return remote(self.fresh.at[1 - self.c], self.other, self.send.at[0], self.recv.at[0], self.sib)

    def result_copy(self):
        return remote(self.mine, self.result.at[self.c], self.send.at[1], self.recv.at[1], self.sib)

    def hop(self, i, first, sending):
        dx, dh = self.HOPS[i]
        s = 1 if sending else -1
        at = moved(moved(self.me, "x", s * dx), "y", 2 * dh)
        g = at[0] * 2 + at[1] // 2
        src, dst = (self.tot, self.arr) if first else (self.car, self.back)
        n = 2 + i + (0 if first else 7)
        return remote(src.at[g], dst.at[self.g if sending else g], self.send.at[n], self.recv.at[n], at)

    def begin(self):
        self.other_copy().start()

    def exchange(self):
        self.other_copy().wait_recv()
        mine_keep = self.keep(lambda b: b == self.block)
        sib_keep = self.keep(lambda b: b == self.sib_block)
        a = jnp.where(self.second, 1.0, sib_keep)
        b = jnp.where(self.second, mine_keep, 1.0)

        def one(g, _):
            self.tot[g] = (
                a * self.fresh[self.c, pl.ds(g * 2, 2)] + b * self.other[pl.ds(g * 2, 2)]
            ).astype(BF)
            return 0

        lax.fori_loop(0, 8, one, 0)
        self.arr[self.g] = self.tot[self.g]
        for i in range(7):
            self.hop(i, True, True).start()

    def sum(self):
        for i in range(7):
            self.hop(i, True, False).wait_recv()
        keeps = [self.keep(lambda b, g=g: b // 2 == g) for g in range(8)]
        order = range(7, -1, -1) if self.backward else range(8)
        carried = jnp.zeros((2, D, D), F32)
        for g in order:
            self.car[g] = carried.astype(BF)
            carried = self.arr[g].astype(F32) + keeps[g] * carried
        self.back[self.g] = self.car[self.g]
        for i in range(7):
            self.hop(i, False, True).start()

    def finish(self):
        for i in range(7):
            self.hop(i, False, False).wait_recv()
        mine_keep = self.keep(lambda b: b == self.block)
        sib_keep = self.keep(lambda b: b == self.sib_block)
        a_mine = jnp.where(self.second, 1.0, 0.0).astype(F32)
        b_mine = jnp.where(self.second, sib_keep, 1.0)
        a_sib = jnp.where(self.second, 0.0, 1.0).astype(F32)
        b_sib = jnp.where(self.second, 1.0, mine_keep)

        def one(g, _):
            two = pl.ds(g * 2, 2)
            entering = self.back[g].astype(F32)
            self.mine[two] = (a_sib * self.fresh[self.c, two] + b_sib * entering).astype(BF)
            self.result[self.c, two] = (a_mine * self.other[two] + b_mine * entering).astype(BF)
            return 0

        lax.fori_loop(0, 8, one, 0)
        self.result_copy().start()

    def result_wait(self):
        at = moved(self.me, "c", 1)
        remote(self.mine, self.result.at[1 - self.c], self.send.at[1], self.recv.at[1], at).wait_recv()

    def drain(self):
        self.other_copy().wait_send()
        self.result_copy().wait_send()
        for i in range(7):
            self.hop(i, True, True).wait_send()
            self.hop(i, False, True).wait_send()


def kernel(
    sb, so, gain, q_in, k_in, v_in, g_in, w_in,
    lay_out, qg_out, kg_out, vg_out, dw_out,
    q, k, v, grad, weight, mask, maskt,
    fresh, other, tot, arr, car, back, mine, inc, outg,
    att, vgl, normed, normed_s, grad_s, agrad, lay,
    part, r1a, r1b, r1c, s2a, s2b, s2c, r2a, r2b, r2c, s3a, s3b, s3c, r3a, r3b, r3c, rows, dwv,
    loc, cs, cr, ags, agr, fws, fwr, scs, scr, sds, sdr, rss, rsr,
):
    me = where_am_i()
    x, y, z, c = me
    sib = moved(me, "c", 1)
    block = lax.axis_index("ctx")
    mine_half = pl.multiple_of(c * HALF, HALF)
    sib_half = pl.multiple_of((1 - c) * HALF, HALF)

    loads = [pltpu.make_async_copy(a, b, loc.at[i]) for i, (a, b) in enumerate(((k_in, k), (v_in, v), (q_in, q), (g_in, grad)))]
    for copy in loads:
        copy.start()

    barrier = pltpu.get_barrier_semaphore()
    partners = [sib] + [moved(me, a, n) for a in "xyz" for n in (1, 2, 3)]
    partners += [moved(moved(me, "x", n), "y", 2) for n in (1, 2, 3)]
    for at in partners:
        pl.semaphore_signal(barrier, inc=1, device_id=device(at), device_id_type=MESH)
    pl.semaphore_wait(barrier, len(partners))

    def chip_rows(core, cols):
        return weight.at[y % 2, z, x, y // 2, pl.ds(pl.multiple_of(core * 16, 16), 16), cols]

    w_local = pltpu.make_async_copy(w_in.at[:, pl.ds(mine_half, HALF)], chip_rows(c, pl.ds(mine_half, HALF)), loc.at[4])
    w_local.start()
    w_cross = remote(w_in.at[:, pl.ds(sib_half, HALF)], chip_rows(c, pl.ds(sib_half, HALF)), cs.at[0], cr.at[0], sib)
    w_cross.start()
    g_cross = remote(g_in.at[:, pl.ds(sib_half, HALF)], grad_s, cs.at[1], cr.at[1], sib)

    def cols_of(core, p):
        return pl.ds(pl.multiple_of(core * HALF + PIECES[p][0], 128), PIECES[p][1])

    def gather(phase, p, n, sending):
        order = PIECES[p][2]
        at = me if sending else moved(me, order[phase], -n)
        view = chips(weight, at, "xyz", order[:phase], cols_of(c, p))
        i = (phase * 3 + p) * 3 + n - 1
        to = moved(me, order[phase], n if sending else -n)
        return remote(view, view, ags.at[i], agr.at[i], to)

    def forward(p, n, sending):
        order = PIECES[p][2]
        at = moved(me, order[2], -n)
        view = chips(weight, at, "xyz", order[:2], cols_of(c if sending else 1 - c, p))
        return remote(view, view, fws.at[p * 4 + n], fwr.at[p * 4 + n], sib)

    lows, highs = [], []
    for s in range(2):
        here = [sb[s, j] == block for j in range(3)]
        starts = [jnp.where(here[j], so[s, j], T) for j in range(3)]
        lows.append(jnp.minimum(jnp.minimum(starts[0], starts[1]), starts[2]))
        lasts = [jnp.where(here[j], so[s, j], 0) for j in range(3)]
        highs.append(jnp.maximum(jnp.maximum(lasts[0], lasts[1]), lasts[2]))
        row = lax.broadcasted_iota(jnp.int32, (T, T), 0)
        col = lax.broadcasted_iota(jnp.int32, (T, T), 1)

        def doc(place):
            return sum((place >= start).astype(jnp.int32) for start in starts)

        same = doc(row) == doc(col)
        mask[s] = jnp.where(same & (row >= col), 1.0, 0.0).astype(F32)
        maskt[s] = jnp.where(same & (col >= row), 1.0, 0.0).astype(F32)

    place = lax.broadcasted_iota(jnp.int32, (T, D), 0)

    def before(s):
        return jnp.where(place < lows[s], 1.0, 0.0).astype(F32)

    def ending(s):
        return jnp.where(place >= highs[s], 1.0, 0.0).astype(F32)

    def tile(ref, s, h):
        return ref[s * T:(s + 1) * T, pl.ds(pl.multiple_of(h * D, D), D)]

    def put(ref, s, h, value):
        ref[s * T:(s + 1) * T, pl.ds(pl.multiple_of(h * D, D), D)] = value

    scan_bufs = (fresh, other, tot, arr, car, back, mine)
    ahead = Scan(me, False, *scan_bufs, inc, scs, scr, sb)
    behind = Scan(me, True, *scan_bufs, outg, sds, sdr, sb)

    loads[0].wait()
    loads[1].wait()

    def kv(s):
        def one(h, _):
            keys = (tile(k, s, h).astype(F32) * ending(s)).astype(BF)
            fresh[s, h] = dot(keys, tile(v, s, h), TN)
            return 0

        lax.fori_loop(0, H, one, 0)

    kv(0)
    kv(1)
    ahead.begin()
    g_cross.start()

    w_local.wait()
    w_cross.wait_recv()
    for p in range(3):
        for n in (1, 2, 3):
            gather(0, p, n, True).start()

    loads[2].wait()

    def intra(s):
        def one(h, _):
            scores = (dot(tile(q, s, h), tile(k, s, h), NT) * mask[s]).astype(BF)
            put(att, s, h, dot(scores, tile(v, s, h), NN))
            return 0

        lax.fori_loop(0, H, one, 0)

    ahead.exchange()
    intra(0)
    for p in range(3):
        for n in (1, 2, 3):
            gather(0, p, n, False).wait_recv()
        for n in (1, 2, 3):
            gather(1, p, n, True).start()
    ahead.sum()
    intra(1)
    for p in range(3):
        for n in (1, 2, 3):
            gather(1, p, n, False).wait_recv()
        for n in (1, 2, 3):
            gather(2, p, n, True).start()
        forward(p, 0, True).start()
    ahead.finish()
    for n in (1, 3, 2):
        for p in range(3):
            gather(2, p, n, False).wait_recv()
            forward(p, n, True).start()
    ahead.result_wait()

    def attend(s):
        def one(h, _):
            out = tile(att, s, h) + before(s) * dot(tile(q, s, h), inc[s, h], NN)
            put(att, s, h, out)
            inv = lax.rsqrt(jnp.mean(out * out, axis=1, keepdims=True) + 1.0)
            put(normed, s, h, (out * inv * gain[pl.ds(h, 1), :]).astype(BF))
            return 0

        lax.fori_loop(0, H, one, 0)

    attend(0)
    attend(1)
    n_cross = remote(normed, normed_s, cs.at[2], cr.at[2], sib)
    n_cross.start()
    loads[3].wait()
    for p in range(3):
        for n in range(4):
            forward(p, n, False).wait_recv()

    def gradient(i, _):
        rows_i = weight[i // 4, i % 4].reshape(2 * D, W)
        for s in range(2):
            back_in = dot(grad[s * T:(s + 1) * T, :], rows_i, NT)
            for j in range(2):
                h = i * 2 + j
                out = tile(att, s, h)
                inv = lax.rsqrt(jnp.mean(out * out, axis=1, keepdims=True) + 1.0)
                scaled = back_in[:, j * D:(j + 1) * D] * gain[pl.ds(h, 1), :]
                inner = jnp.mean(scaled * out, axis=1, keepdims=True)
                ag = (inv * (scaled - out * (inv * inv * inner))).astype(BF)
                put(agrad, s, h, ag)
                queries = (tile(q, s, h).astype(F32) * before(s)).astype(BF)
                fresh[s, h] = dot(queries, ag, TN)
        return 0

    ahead.drain()
    lax.fori_loop(0, 8, gradient, 0)
    behind.begin()

    r1, s2, r2 = (r1a, r1b, r1c), (s2a, s2b, s2c), (r2a, r2b, r2c)
    s3, r3 = (s3a, s3b, s3c), (r3a, r3b, r3c)

    def spread(phase, p, n, sending):
        order = PIECES[p][2][::-1]
        to = moved(me, order[phase], n if sending else -n)
        i = (phase * 3 + p) * 3 + n - 1
        free = order[phase + 1:]
        if phase == 0:
            src = chips(part, to, "xyz", free, pl.ds(PIECES[p][0], PIECES[p][1]))
        else:
            src = chips((s2, s3)[phase - 1][p], to, order[phase:], free)
        dst = (r1, r2, r3)[phase][p].at[n - 1]
        return remote(src, dst, rss.at[i], rsr.at[i], to)

    g_cross.wait_recv()
    n_cross.wait_recv()
    for p in range(3):
        first, width, _ = PIECES[p]

        def product(i, _):
            feats = pl.ds(pl.multiple_of(i * 2 * D, 2 * D), 2 * D)
            mine_cols = pl.ds(pl.multiple_of(c * HALF + first, 128), width)
            total = dot(normed[:, feats], grad[:, mine_cols], TN)
            total += dot(normed_s[:, feats], grad_s[:, first:first + width], TN)
            part[i // 4, i % 4, :, :, :, first:first + width] = total.astype(BF).reshape(4, 2, 32, width)
            return 0

        lax.fori_loop(0, 8, product, 0)
        for n in (1, 2, 3):
            spread(0, p, n, True).start()
        if p == 0:
            behind.exchange()

    def project(n, _):
        cols = pl.ds(pl.multiple_of(n * 256, 256), 256)
        lay[:, cols] = dot(normed[...], weight[:, :, :, :, :, cols].reshape(W, 256), NN).astype(BF)
        return 0

    lax.fori_loop(0, 4, project, 0)
    behind.sum()
    lax.fori_loop(4, 8, project, 0)
    lay_copy = pltpu.make_async_copy(lay, lay_out, loc.at[5])
    lay_copy.start()

    def add_up(phase, p):
        order = PIECES[p][2][::-1]
        width = PIECES[p][1]
        for n in (1, 2, 3):
            spread(phase, p, n, False).wait_recv()
        free = order[phase + 1:]
        if phase == 0:
            own = chips(part, me, "xyz", free, pl.ds(PIECES[p][0], width))
        else:
            own = chips((s2, s3)[phase - 1][p], me, order[phase:], free)
        got = (r1, r2, r3)[phase][p]
        dims = set_dims(free)
        if phase == 2:
            total = own[...].astype(F32)
            for n in range(3):
                total += got[n].astype(F32)
            rows[:, PIECES[p][0]:PIECES[p][0] + width] = total
            return
        target = (s2, s3)[phase][p]

        def one(i, _):
            lead, rest = [], i
            for d in dims[::-1]:
                lead = [rest % d] + lead
                rest = rest // d
            lead = tuple(lead)
            total = own[lead].astype(F32)
            for n in range(3):
                total += got[(n,) + lead].astype(F32)
            target[lead] = total.astype(target.dtype)
            return 0

        lax.fori_loop(0, math.prod(dims), one, 0)

    def local_grads(s):
        def one(h, _):
            qh, kh, vh, ah = tile(q, s, h), tile(k, s, h), tile(v, s, h), tile(agrad, s, h)
            ds = (dot(ah, vh, NT) * mask[s]).astype(BF)
            dst = (dot(vh, ah, NT) * maskt[s]).astype(BF)
            st = (dot(kh, qh, NT) * maskt[s]).astype(BF)
            put(att, s, h, dot(dst, qh, NN))
            put(vgl, s, h, dot(st, ah, NN))
            qg = dot(ds, kh, NN) + before(s) * dot(ah, inc[s, h], NT)
            put(q, s, h, qg.astype(BF))
            return 0

        lax.fori_loop(0, H, one, 0)

    local_grads(0)
    behind.finish()
    for p in range(3):
        add_up(0, p)
        for n in (1, 2, 3):
            spread(1, p, n, True).start()
    local_grads(1)
    q_copy = pltpu.make_async_copy(q, qg_out, loc.at[6])
    q_copy.start()
    for p in range(3):
        add_up(1, p)
        for n in (1, 2, 3):
            spread(2, p, n, True).start()
    behind.result_wait()

    def final(s):
        def one(h, _):
            kh, vh, out = tile(k, s, h), tile(v, s, h), outg[s, h]
            kg = tile(att, s, h) + ending(s) * dot(vh, out, NT)
            vg = tile(vgl, s, h) + ending(s) * dot(kh, out, NN)
            put(k, s, h, kg.astype(BF))
            put(v, s, h, vg.astype(BF))
            return 0

        lax.fori_loop(0, H, one, 0)

    final(0)
    final(1)
    k_copy = pltpu.make_async_copy(k, kg_out, loc.at[7])
    k_copy.start()
    v_copy = pltpu.make_async_copy(v, vg_out, loc.at[8])
    v_copy.start()
    for p in range(3):
        add_up(2, p)
    mine_rows = pl.ds(pl.multiple_of(c * 16, 16), 16)
    sib_rows = pl.ds(pl.multiple_of((1 - c) * 16, 16), 16)
    rows[...] = rows[...] * (1.0 / 256.0)
    d_cross = remote(rows.at[sib_rows], dwv.at[:, pl.ds(mine_half, HALF)], cs.at[3], cr.at[3], sib)
    d_cross.start()
    dwv[:, pl.ds(mine_half, HALF)] = rows[mine_rows, :]
    d_back = remote(rows.at[sib_rows], dwv.at[:, pl.ds(sib_half, HALF)], cs.at[3], cr.at[3], sib)
    d_back.wait_recv()
    d_copy = pltpu.make_async_copy(dwv, dw_out, loc.at[9])
    d_copy.start()

    for copy in (w_cross, g_cross, n_cross, d_cross):
        copy.wait_send()
    for p in range(3):
        for n in range(4):
            forward(p, n, True).wait_send()
        for phase in range(3):
            for n in (1, 2, 3):
                gather(phase, p, n, True).wait_send()
                spread(phase, p, n, True).wait_send()
    behind.drain()
    for copy in (lay_copy, q_copy, k_copy, v_copy, d_copy):
        copy.wait()


def per_device(query_rows, key_rows, value_rows, out_grad, norm_gain, out_weight, start_block, start_offset):
    flat = (2 * T, W)
    state = (H, D, D)
    paired = (8, 2, D, D)
    vm = lambda shape, kind: pltpu.VMEM(shape, kind)
    any_space = pl.BlockSpec(memory_space=pl.ANY)
    orders = [(p[2][::-1], p[1]) for p in PIECES]
    r1 = [vm((3,) + set_dims(o[1:]) + (32, w), BF) for o, w in orders]
    s2 = [vm(set_dims(o[1:]) + (32, w), BF) for o, w in orders]
    r2 = [vm((3,) + set_dims(o[2:]) + (32, w), BF) for o, w in orders]
    s3 = [vm(set_dims(o[2:]) + (32, w), F32) for o, w in orders]
    r3 = [vm((3, 32, w), F32) for o, w in orders]
    dma = pltpu.SemaphoreType.DMA
    scratch = (
        [vm(flat, BF)] * 4
        + [vm((2, 4, 4, 2, 32, W), BF), vm((2, T, T), F32), vm((2, T, T), F32)]
        + [vm((2,) + state, F32), vm(state, F32)]
        + [vm(paired, BF)] * 4
        + [vm(state, BF), vm((2,) + state, BF), vm((2,) + state, BF)]
        + [vm(flat, F32), vm(flat, F32), vm(flat, BF), vm(flat, BF), vm((2 * T, HALF), BF), vm(flat, BF), vm(flat, BF)]
        + [vm((2, 4, 4, 2, 32, HALF), BF)]
        + r1 + s2 + r2 + s3 + r3
        + [vm((32, HALF), F32), vm((16, W), F32)]
        + [dma((10,)), dma((4,)), dma((4,)), dma((27,)), dma((27,)), dma((12,)), dma((12,))]
        + [dma((16,)), dma((16,)), dma((16,)), dma((16,)), dma((27,)), dma((27,))]
    )
    smem = pl.BlockSpec(memory_space=pltpu.SMEM)
    outs = pl.pallas_call(
        kernel,
        name="linear_attention",
        out_shape=[jax.ShapeDtypeStruct(flat, BF)] * 4 + [jax.ShapeDtypeStruct((16, W), F32)],
        in_specs=[smem, smem, pl.BlockSpec(memory_space=pltpu.VMEM)] + [any_space] * 5,
        out_specs=[any_space] * 5,
        scratch_shapes=scratch,
        compiler_params=pltpu.CompilerParams(
            collective_id=0, has_side_effects=True, vmem_limit_bytes=60 * 1024 * 1024
        ),
    )(
        start_block, start_offset, norm_gain,
        query_rows.reshape(flat), key_rows.reshape(flat), value_rows.reshape(flat), out_grad.reshape(flat),
        out_weight,
    )
    shape = query_rows.shape
    return tuple(o.reshape(shape) for o in outs[:4]) + (outs[4],)


def solution(mesh):
    rows = P("dp", "ctx", None)
    spread = P(("dp", "ctx"), None)
    return jax.shard_map(
        per_device,
        mesh=mesh,
        in_specs=(rows, rows, rows, rows, P(), spread, P("dp", None), P("dp", None)),
        out_specs=(rows, rows, rows, rows, spread),
        check_vma=False,
    )
```

time: 1420 us -> 146 us (0.10)
  waiting for transfers between devices: 1140 us -> 0 us
  Pallas kernels: 0 us -> 136 us
  other arithmetic: 114 us -> 0 us
  matrix products: 80 us -> 0 us
  blocking collectives: 34.3 us -> 0 us
  local copies, waits for them, and re-layouts: 36 us -> 9.98 us
    reduce_scatter x1 -> x0, waiting for transfers between devices: 626 us -> none  [per_device(): lax.psum_scatter(lax.dot_general(flat_normed, flat_grad, contract_rows, p...]
    all_gather x3 -> x0, waiting for transfers between devices: 513 us -> none  [the longest x2 370 us: entering(): everything = jax.tree.map(lambda part: lax.all_gather(part, axis), value)]
    pallas_call x0 -> x1, Pallas kernels: none -> 136 us  [per_device(): pl.pallas_call(kernel, name='linear_attention', out_shape=[jax.ShapeDtype...]
    select_n x32 -> x0, other arithmetic: 106 us -> none  [hop(): return jax.tree.map(lambda a, b: jnp.where(reached, a, b), new, before)]
    dot_general x15 -> x0, matrix products: 80 us -> none  [the longest x1 9.86 us: per_device(): lax.dot_general(flat_normed, flat_grad, contract_rows, preferred_element_...]
    unnamed x1 -> x0, blocking collectives: 34.3 us -> none
  transfers between devices with their start and end apart: 4 -> 0, of which waited for: 4 -> 0; matrix products, arithmetic and copies ran while one was open for 5% -> 0% of each run, Pallas kernels for 0% -> 0%
where the time goes in v1:
time: 146 us
  Pallas kernels  136 us (93%)
  local copies, waits for them, and re-layouts  9.98 us (7%)
    pallas_call x1, Pallas kernels, per_device(): pl.pallas_call(kernel, name='linear_attention', out_shape=[jax.ShapeDtype...  136 us
    unnamed x13, local copies, waits for them, and re-layouts  9.98 us

profile of v1, /device:TPU:1, one launch (start us, length us, event | category | flops | bytes accessed | tf_op | source)
XLA Modules:
  0.0 146.2 jit_solution(16315817256651628304)
XLA Ops:
  0.6 135.6 %linear_attention.1 = (bf16[512,2048]{1,0:T(8,128)(2,1)}, bf16[512,2048]{1,0:T(8,128)(2,1)}, bf16[512,2048]{1,0:T(8,128)(2,1)}, bf16[512,2048]{1,0:T(8,128)(2,1)}, f32[16,2048]{1,0:T(8,128)}) custom-call(s32[2,3]{1,0:T(2,128)} %sb.1, s32[2,3]{1,0:T(2,128)} %so.1, f32[16,128]{1,0:T(8,128)} %gain.1, bf16[512,2048]{1,0:T(8,128)(2,1)} %bitcast.12, ...), custom_call_target="tpu_custom_call" | custom-call | tf_op jit(solution)/shard_map/linear_attention/pallas_call | solution.py:525
  136.2 0.0 copy-start.2
  136.2 3.3 %copy.18 = bf16[2,256,2048]{2,1,0:T(8,128)(2,1)} copy(bf16[2,256,2048]{2,1,0:T(8,128)(2,1)} %bitcast.11) | data formatting | bytes 4194304
  139.5 0.0 copy-done.2
  139.5 0.0 copy-start.1
  139.5 1.3 copy.19
  140.9 1.0 copy-done.1
  141.9 0.0 copy-start
  141.9 1.3 copy.20
  143.2 1.0 copy-done
  144.2 0.0 copy-start.3
  144.2 1.3 copy.21
  145.6 0.0 copy-done.3
  145.6 0.7 copy.22
Async XLA Ops:
  136.2 3.3 %copy-start.2 = (bf16[512,2048]{1,0:T(8,128)(2,1)S(1)}, bf16[512,2048]{1,0:T(8,128)(2,1)}, u32[]{:S(2)}) copy-start(bf16[512,2048]{1,0:T(8,128)(2,1)} %get-tuple-element.11) | copy-start | bytes 6291460
  139.5 2.3 %copy-start.1 = (bf16[512,2048]{1,0:T(8,128)(2,1)S(1)}, bf16[512,2048]{1,0:T(8,128)(2,1)}, u32[]{:S(2)}) copy-start(bf16[512,2048]{1,0:T(8,128)(2,1)} %get-tuple-element.12) | copy-start | bytes 6291460
  141.9 2.3 %copy-start = (bf16[512,2048]{1,0:T(8,128)(2,1)S(1)}, bf16[512,2048]{1,0:T(8,128)(2,1)}, u32[]{:S(2)}) copy-start(bf16[512,2048]{1,0:T(8,128)(2,1)} %get-tuple-element.13) | copy-start | bytes 6291460
  144.2 1.3 copy-start.3

commit v2 on v1

v2 whole, which is shorter than its diff:
```python
import functools
import math

import jax
import jax.numpy as jnp
from jax import lax
from jax.experimental import pallas as pl
from jax.experimental.pallas import tpu as pltpu
from jax.sharding import PartitionSpec as P

BF, F32 = jnp.bfloat16, jnp.float32
MESH = pl.DeviceIdType.MESH
T, H, D, W = 256, 16, 128, 2048
HALF = W // 2
PIECES = ((0, 384, "yxz"), (384, 384, "zyx"), (768, 256, "xzy"))
NT = (((1,), (1,)), ((), ()))
TN = (((0,), (0,)), ((), ()))
NN = (((1,), (0,)), ((), ()))


def dot(a, b, dims):
    return lax.dot_general(a, b, dims, preferred_element_type=F32)


def where_am_i():
    dp, ctx = lax.axis_index("dp"), lax.axis_index("ctx")
    return (ctx // 4, 2 * ((ctx // 2) % 2) + dp // 4, dp % 4, ctx % 2)


def device(at):
    x, y, z, c = at
    return ((y % 2) * 4 + z, (x * 2 + y // 2) * 2 + c)


def moved(at, axis, k):
    x, y, z, c = at
    if axis == "x":
        return ((x + k) % 4, y, z, c)
    if axis == "y":
        return (x, (y + k) % 4, z, c)
    if axis == "z":
        return (x, y, (z + k) % 4, c)
    return (x, y, z, 1 - c)


def chips(ref, at, held, free, cols=None, lead=()):
    x, y, z, _ = at
    every = slice(None)
    parts = (("y", y % 2), ("z", z), ("x", x), ("y", y // 2))
    index = tuple(every if axis in free else place for axis, place in parts if axis in held)
    tail = (every,) if cols is None else (every, cols)
    return ref.at[tuple(lead) + index + tail]


def set_dims(held):
    return tuple(n for axis, n in (("y", 2), ("z", 4), ("x", 4), ("y", 2)) if axis in held)


def remote(src, dst, ssem, rsem, at):
    return pltpu.make_async_remote_copy(
        src_ref=src, dst_ref=dst, send_sem=ssem, recv_sem=rsem, device_id=device(at), device_id_type=MESH
    )


class Scan:
    HOPS = tuple((dx, dh) for dx in range(4) for dh in range(2) if dx or dh)

    def __init__(self, me, backward, half, fresh, other, tot, arr, car, back, mine, result, send, recv, sb):
        self.me, self.backward, self.half = me, backward, half
        self.fresh, self.other, self.tot, self.arr = fresh, other, tot, arr
        self.car, self.back, self.mine, self.result = car, back, mine, result
        self.send, self.recv, self.sb = send, recv, sb
        x, y, _, c = me
        self.c, self.g = c, x * 2 + y // 2
        self.sib = moved(me, "c", 1)
        self.block = self.g * 2 + c
        self.sib_block = self.g * 2 + 1 - c
        self.second = (c == 0) if backward else (c == 1)
        self.heads = pl.ds(half * 8, 8)

    def keep(self, test):
        hit = test(self.sb[self.c, 0]) | test(self.sb[self.c, 1]) | test(self.sb[self.c, 2])
        return jnp.where(hit, 0.0, 1.0).astype(F32)

    def pair(self, src, dst, n):
        n += 16 * self.half
        return remote(src, dst, self.send.at[n], self.recv.at[n], self.sib)

    def other_copy(self):
        return self.pair(self.fresh.at[1 - self.c, self.heads], self.other.at[self.heads], 0)

    def result_copy(self, row):
        return self.pair(self.mine.at[self.heads], self.result.at[row, self.heads], 1)

    def hop(self, i, first, sending):
        dx, dh = self.HOPS[i]
        s = 1 if sending else -1
        at = moved(moved(self.me, "x", s * dx), "y", 2 * dh)
        g = at[0] * 2 + at[1] // 2
        src, dst = (self.tot, self.arr) if first else (self.car, self.back)
        n = 16 * self.half + 2 + i + (0 if first else 7)
        return remote(
            src.at[self.half, g], dst.at[self.half, self.g if sending else g], self.send.at[n], self.recv.at[n], at
        )

    def begin(self):
        self.other_copy().start()

    def exchange(self):
        self.other_copy().wait_recv()
        mine_keep = self.keep(lambda b: b == self.block)
        sib_keep = self.keep(lambda b: b == self.sib_block)
        a = jnp.where(self.second, 1.0, sib_keep)
        b = jnp.where(self.second, mine_keep, 1.0)

        def one(i, _):
            for g in (i * 2, i * 2 + 1):
                h = self.half * 8 + g
                self.tot[self.half, g] = (a * self.fresh[self.c, h] + b * self.other[h]).astype(BF)
            return 0

        lax.fori_loop(0, 4, one, 0)
        self.arr[self.half, self.g] = self.tot[self.half, self.g]
        for i in range(7):
            self.hop(i, True, True).start()

    def sum(self):
        for i in range(7):
            self.hop(i, True, False).wait_recv()
        keeps = [self.keep(lambda b, g=g: b // 2 == g) for g in range(8)]
        order = range(7, -1, -1) if self.backward else range(8)
        carried = jnp.zeros((D, D), F32)
        for g in order:
            self.car[self.half, g] = carried.astype(BF)
            carried = self.arr[self.half, g].astype(F32) + keeps[g] * carried
        self.back[self.half, self.g] = self.car[self.half, self.g]
        for i in range(7):
            self.hop(i, False, True).start()

    def finish(self):
        for i in range(7):
            self.hop(i, False, False).wait_recv()
        mine_keep = self.keep(lambda b: b == self.block)
        sib_keep = self.keep(lambda b: b == self.sib_block)
        a_mine = jnp.where(self.second, 1.0, 0.0).astype(F32)
        b_mine = jnp.where(self.second, sib_keep, 1.0)
        a_sib = jnp.where(self.second, 0.0, 1.0).astype(F32)
        b_sib = jnp.where(self.second, 1.0, mine_keep)

        def one(i, _):
            for g in (i * 2, i * 2 + 1):
                h = self.half * 8 + g
                entering = self.back[self.half, g].astype(F32)
                self.mine[h] = (a_sib * self.fresh[self.c, h] + b_sib * entering).astype(BF)
                self.result[self.c, h] = (a_mine * self.other[h] + b_mine * entering).astype(BF)
            return 0

        lax.fori_loop(0, 4, one, 0)
        self.result_copy(self.c).start()

    def result_wait(self):
        self.result_copy(1 - self.c).wait_recv()

    def drain(self):
        self.other_copy().wait_send()
        self.result_copy(self.c).wait_send()
        for i in range(7):
            self.hop(i, True, True).wait_send()
            self.hop(i, False, True).wait_send()


def kernel(
    sb, so, gain, q_in, k_in, v_in, g_in, w_in,
    lay, q, k, v, dwv,
    grad, weight, mask, maskt,
    fresh, other, tot, arr, car, back, mine, inc, outg,
    att, vgl, normed, nt, nts, grad_s, agrad,
    part, r1a, r1b, r1c, s2a, s2b, s2c, r2a, r2b, r2c, s3a, s3b, s3c, r3a, r3b, r3c, rows,
    loc, cs, cr, ags, agr, fws, fwr, scs, scr, sds, sdr, rss, rsr,
):
    me = where_am_i()
    x, y, z, c = me
    sib = moved(me, "c", 1)
    block = lax.axis_index("ctx")
    mine_half = pl.multiple_of(c * HALF, HALF)
    sib_half = pl.multiple_of((1 - c) * HALF, HALF)

    loads = [pltpu.make_async_copy(a, b, loc.at[i]) for i, (a, b) in enumerate(((k_in, k), (v_in, v), (q_in, q), (g_in, grad)))]
    for copy in loads:
        copy.start()

    barrier = pltpu.get_barrier_semaphore()
    partners = [sib] + [moved(me, a, n) for a in "xyz" for n in (1, 2, 3)]
    partners += [moved(moved(me, "x", n), "y", 2) for n in (1, 2, 3)]
    for at in partners:
        pl.semaphore_signal(barrier, inc=1, device_id=device(at), device_id_type=MESH)

    def chip_rows(core, cols):
        return weight.at[y % 2, z, x, y // 2, pl.ds(pl.multiple_of(core * 16, 16), 16), cols]

    w_local = pltpu.make_async_copy(w_in.at[:, pl.ds(mine_half, HALF)], chip_rows(c, pl.ds(mine_half, HALF)), loc.at[4])
    w_local.start()

    def cols_of(core, p):
        return pl.ds(pl.multiple_of(core * HALF + PIECES[p][0], 128), PIECES[p][1])

    def gather(phase, p, n, sending):
        order = PIECES[p][2]
        at = me if sending else moved(me, order[phase], -n)
        view = chips(weight, at, "xyz", order[:phase], cols_of(c, p))
        i = (phase * 3 + p) * 3 + n - 1
        to = moved(me, order[phase], n if sending else -n)
        return remote(view, view, ags.at[i], agr.at[i], to)

    def forward(p, n, sending):
        order = PIECES[p][2]
        at = moved(me, order[2], -n)
        view = chips(weight, at, "xyz", order[:2], cols_of(c if sending else 1 - c, p))
        return remote(view, view, fws.at[p * 4 + n], fwr.at[p * 4 + n], sib)

    lows, highs = [], []
    for s in range(2):
        here = [sb[s, j] == block for j in range(3)]
        starts = [jnp.where(here[j], so[s, j], T) for j in range(3)]
        lows.append(jnp.minimum(jnp.minimum(starts[0], starts[1]), starts[2]))
        lasts = [jnp.where(here[j], so[s, j], 0) for j in range(3)]
        highs.append(jnp.maximum(jnp.maximum(lasts[0], lasts[1]), lasts[2]))
        row = lax.broadcasted_iota(jnp.int32, (T, T), 0)
        col = lax.broadcasted_iota(jnp.int32, (T, T), 1)

        def doc(place):
            return sum((place >= start).astype(jnp.int32) for start in starts)

        same = doc(row) == doc(col)
        mask[s] = jnp.where(same & (row >= col), 1.0, 0.0).astype(F32)
        maskt[s] = jnp.where(same & (col >= row), 1.0, 0.0).astype(F32)

    place = lax.broadcasted_iota(jnp.int32, (T, D), 0)

    def before(s):
        return jnp.where(place < lows[s], 1.0, 0.0).astype(F32)

    def ending(s):
        return jnp.where(place >= highs[s], 1.0, 0.0).astype(F32)

    def tile(ref, s, h):
        return ref[s * T:(s + 1) * T, pl.ds(pl.multiple_of(h * D, D), D)]

    def put(ref, s, h, value):
        ref[s * T:(s + 1) * T, pl.ds(pl.multiple_of(h * D, D), D)] = value

    def over(first, last, step, body):
        def one(i, _):
            body([(s, first + i * step + j) for j in range(step) for s in range(2)])
            return 0

        lax.fori_loop(0, (last - first) // step, one, 0)

    scan_bufs = (fresh, other, tot, arr, car, back, mine)
    ahead = [Scan(me, False, i, *scan_bufs, inc, scs, scr, sb) for i in range(2)]
    behind = [Scan(me, True, i, *scan_bufs, outg, sds, sdr, sb) for i in range(2)]

    def kv(todo):
        keys = [(tile(k, s, h).astype(F32) * ending(s)).astype(BF) for s, h in todo]
        states = [dot(a, tile(v, s, h), TN) for a, (s, h) in zip(keys, todo)]
        for a, (s, h) in zip(states, todo):
            fresh[s, h] = a

    def intra(todo):
        scores = [dot(tile(q, s, h), tile(k, s, h), NT) for s, h in todo]
        scores = [(a * mask[s]).astype(BF) for a, (s, h) in zip(scores, todo)]
        outs = [dot(a, tile(v, s, h), NN) for a, (s, h) in zip(scores, todo)]
        for a, (s, h) in zip(outs, todo):
            put(att, s, h, a)

    def attend(todo):
        outs = [dot(tile(q, s, h), inc[s, h], NN) for s, h in todo]
        outs = [tile(att, s, h) + before(s) * a for a, (s, h) in zip(outs, todo)]
        invs = [lax.rsqrt(jnp.mean(a * a, axis=1, keepdims=True) + 1.0) for a in outs]
        norm = [a * i * gain[pl.ds(h, 1), :] for a, i, (s, h) in zip(outs, invs, todo)]
        for a, n, (s, h) in zip(outs, norm, todo):
            put(att, s, h, a)
            put(normed, s, h, n.astype(BF))
            nt[pl.ds(pl.multiple_of(h * D, D), D), s * T:(s + 1) * T] = n.T.astype(BF)

    def n_cross(half):
        view = pl.ds(half * HALF, HALF)
        return remote(nt.at[view], nts.at[view], cs.at[2 + half], cr.at[2 + half], sib)

    def gradient(i, _):
        rows_i = weight[i // 4, i % 4].reshape(2 * D, W)
        back_in = dot(grad[...], rows_i, NT)
        todo = [(s, j) for j in range(2) for s in range(2)]
        outs = [tile(att, s, i * 2 + j) for s, j in todo]
        invs = [lax.rsqrt(jnp.mean(a * a, axis=1, keepdims=True) + 1.0) for a in outs]
        scaled = [back_in[s * T:(s + 1) * T, j * D:(j + 1) * D] * gain[pl.ds(i * 2 + j, 1), :] for s, j in todo]
        inner = [jnp.mean(a * b, axis=1, keepdims=True) for a, b in zip(scaled, outs)]
        ags_ = [(v_ * (a - b * (v_ * v_ * n))).astype(BF) for v_, a, b, n in zip(invs, scaled, outs, inner)]
        queries = [(tile(q, s, i * 2 + j).astype(F32) * before(s)).astype(BF) for s, j in todo]
        states = [dot(a, b, TN) for a, b in zip(queries, ags_)]
        for a, b, (s, j) in zip(ags_, states, todo):
            put(agrad, s, i * 2 + j, a)
            fresh[s, i * 2 + j] = b
        return 0

    r1, s2, r2 = (r1a, r1b, r1c), (s2a, s2b, s2c), (r2a, r2b, r2c)
    s3, r3 = (s3a, s3b, s3c), (r3a, r3b, r3c)

    def spread(phase, p, n, sending):
        order = PIECES[p][2][::-1]
        to = moved(me, order[phase], n if sending else -n)
        i = (phase * 3 + p) * 3 + n - 1
        free = order[phase + 1:]
        if phase == 0:
            src = chips(part, to, "xyz", free, pl.ds(PIECES[p][0], PIECES[p][1]))
        else:
            src = chips((s2, s3)[phase - 1][p], to, order[phase:], free)
        dst = (r1, r2, r3)[phase][p].at[n - 1]
        return remote(src, dst, rss.at[i], rsr.at[i], to)

    def product(p):
        first, width, _ = PIECES[p]

        def one(i, _):
            feats = pl.ds(pl.multiple_of(i * 512, 512), 512)
            mine_cols = pl.ds(pl.multiple_of(c * HALF + first, 128), width)
            total = dot(nt[feats, :], grad[:, mine_cols], NN)
            total += dot(nts[feats, :], grad_s[:, first:first + width], NN)
            total = total.astype(BF).reshape(2, 4, 2, 32, width)
            for j in range(2):
                part[i // 2, (i % 2) * 2 + j, :, :, :, first:first + width] = total[j]
            return 0

        lax.fori_loop(0, 4, one, 0)
        for n in (1, 2, 3):
            spread(0, p, n, True).start()

    def project(n, _):
        cols = pl.ds(pl.multiple_of(n * 256, 256), 256)
        lay[:, cols] = dot(normed[...], weight[:, :, :, :, :, cols].reshape(W, 256), NN).astype(BF)
        return 0

    def add_up(phase, p):
        order = PIECES[p][2][::-1]
        width = PIECES[p][1]
        for n in (1, 2, 3):
            spread(phase, p, n, False).wait_recv()
        free = order[phase + 1:]
        if phase == 0:
            own = chips(part, me, "xyz", free, pl.ds(PIECES[p][0], width))
        else:
            own = chips((s2, s3)[phase - 1][p], me, order[phase:], free)
        got = (r1, r2, r3)[phase][p]
        dims = set_dims(free)
        if phase == 2:
            total = own[...].astype(F32)
            for n in range(3):
                total += got[n].astype(F32)
            rows[:, PIECES[p][0]:PIECES[p][0] + width] = total * (1.0 / 256.0)
            return
        target = (s2, s3)[phase][p]

        def one(i, _):
            lead, rest = [], i
            for d in dims[::-1]:
                lead = [rest % d] + lead
                rest = rest // d
            lead = tuple(lead)
            total = own[lead].astype(F32)
            for n in range(3):
                total += got[(n,) + lead].astype(F32)
            target[lead] = total.astype(target.dtype)
            return 0

        lax.fori_loop(0, math.prod(dims), one, 0)
        for n in (1, 2, 3):
            spread(phase + 1, p, n, True).start()

    def local_grads(todo):
        ql, kl = [tile(q, s, h) for s, h in todo], [tile(k, s, h) for s, h in todo]
        vl, al = [tile(v, s, h) for s, h in todo], [tile(agrad, s, h) for s, h in todo]
        ds = [dot(a, b, NT) for a, b in zip(al, vl)]
        dst = [dot(b, a, NT) for a, b in zip(al, vl)]
        st = [dot(b, a, NT) for a, b in zip(ql, kl)]
        far = [dot(a, inc[s, h], NT) for a, (s, h) in zip(al, todo)]
        ds = [(a * mask[s]).astype(BF) for a, (s, h) in zip(ds, todo)]
        dst = [(a * maskt[s]).astype(BF) for a, (s, h) in zip(dst, todo)]
        st = [(a * maskt[s]).astype(BF) for a, (s, h) in zip(st, todo)]
        kg = [dot(a, b, NN) for a, b in zip(dst, ql)]
        vg = [dot(a, b, NN) for a, b in zip(st, al)]
        qg = [dot(a, b, NN) + before(s) * f for a, b, f, (s, h) in zip(ds, kl, far, todo)]
        for i, (s, h) in enumerate(todo):
            put(att, s, h, kg[i])
            put(vgl, s, h, vg[i])
            put(q, s, h, qg[i].astype(BF))

    def final(todo):
        kl, vl = [tile(k, s, h) for s, h in todo], [tile(v, s, h) for s, h in todo]
        kg = [dot(a, outg[s, h], NT) for a, (s, h) in zip(vl, todo)]
        vg = [dot(a, outg[s, h], NN) for a, (s, h) in zip(kl, todo)]
        kg = [tile(att, s, h) + ending(s) * a for a, (s, h) in zip(kg, todo)]
        vg = [tile(vgl, s, h) + ending(s) * a for a, (s, h) in zip(vg, todo)]
        for i, (s, h) in enumerate(todo):
            put(k, s, h, kg[i].astype(BF))
            put(v, s, h, vg[i].astype(BF))

    w_cross = remote(w_in.at[:, pl.ds(sib_half, HALF)], chip_rows(c, pl.ds(sib_half, HALF)), cs.at[0], cr.at[0], sib)
    g_cross = remote(g_in.at[:, pl.ds(sib_half, HALF)], grad_s, cs.at[1], cr.at[1], sib)

    def passed(n):
        for p in range(3):
            gather(2, p, n, False).wait_recv()
            forward(p, n, True).start()

    pl.semaphore_wait(barrier, len(partners))
    w_cross.start()
    loads[0].wait()
    loads[1].wait()
    over(0, 8, 2, kv)
    ahead[0].begin()
    w_local.wait()
    w_cross.wait_recv()
    for p in range(3):
        for n in (1, 2, 3):
            gather(0, p, n, True).start()
    over(8, 16, 2, kv)
    ahead[1].begin()
    ahead[0].exchange()
    ahead[1].exchange()
    g_cross.start()
    loads[2].wait()
    over(0, 8, 2, intra)
    for p in range(3):
        for n in (1, 2, 3):
            gather(0, p, n, False).wait_recv()
        for n in (1, 2, 3):
            gather(1, p, n, True).start()
    ahead[0].sum()
    ahead[1].sum()
    over(8, 16, 2, intra)
    for p in range(3):
        for n in (1, 2, 3):
            gather(1, p, n, False).wait_recv()
        for n in (1, 2, 3):
            gather(2, p, n, True).start()
        forward(p, 0, True).start()
    ahead[0].finish()
    ahead[1].finish()
    ahead[0].result_wait()
    over(0, 8, 2, attend)
    n_cross(0).start()
    ahead[1].result_wait()
    over(8, 16, 2, attend)
    n_cross(1).start()
    passed(1)
    loads[3].wait()
    g_cross.wait_recv()
    n_cross(0).wait_recv()
    n_cross(1).wait_recv()
    product(0)
    passed(3)
    product(1)
    passed(2)
    product(2)
    for scan in ahead:
        scan.drain()
    for p in range(3):
        for n in range(4):
            forward(p, n, False).wait_recv()
    lax.fori_loop(0, 4, gradient, 0)
    behind[0].begin()
    lax.fori_loop(4, 8, gradient, 0)
    behind[1].begin()
    behind[0].exchange()
    lax.fori_loop(0, 2, project, 0)
    behind[1].exchange()
    for p in range(3):
        add_up(0, p)
    lax.fori_loop(2, 8, project, 0)
    behind[0].sum()
    behind[1].sum()
    over(0, 8, 2, local_grads)
    for p in range(3):
        add_up(1, p)
    behind[0].finish()
    behind[1].finish()
    over(8, 16, 2, local_grads)
    for p in range(3):
        add_up(2, p)
    mine_rows = pl.ds(pl.multiple_of(c * 16, 16), 16)
    sib_rows = pl.ds(pl.multiple_of((1 - c) * 16, 16), 16)
    d_cross = remote(rows.at[sib_rows], dwv.at[:, pl.ds(mine_half, HALF)], cs.at[4], cr.at[4], sib)
    d_back = remote(rows.at[sib_rows], dwv.at[:, pl.ds(sib_half, HALF)], cs.at[4], cr.at[4], sib)
    d_cross.start()
    dwv[:, pl.ds(mine_half, HALF)] = rows[mine_rows, :]
    behind[0].result_wait()
    over(0, 8, 2, final)
    behind[1].result_wait()
    over(8, 16, 2, final)
    d_back.wait_recv()

    for copy in (w_cross, g_cross, n_cross(0), n_cross(1), d_cross):
        copy.wait_send()
    for p in range(3):
        for n in range(4):
            forward(p, n, True).wait_send()
        for phase in range(3):
            for n in (1, 2, 3):
                gather(phase, p, n, True).wait_send()
                spread(phase, p, n, True).wait_send()
    for scan in behind:
        scan.drain()


def per_device(query_rows, key_rows, value_rows, out_grad, norm_gain, out_weight, start_block, start_offset):
    flat = (2 * T, W)
    state = (H, D, D)
    paired = (2, 8, D, D)
    vm = pltpu.VMEM
    any_space = pl.BlockSpec(memory_space=pl.ANY)
    in_vmem = pl.BlockSpec(memory_space=pltpu.VMEM)
    orders = [(p[2][::-1], p[1]) for p in PIECES]
    r1 = [vm((3,) + set_dims(o[1:]) + (32, w), BF) for o, w in orders]
    s2 = [vm(set_dims(o[1:]) + (32, w), BF) for o, w in orders]
    r2 = [vm((3,) + set_dims(o[2:]) + (32, w), BF) for o, w in orders]
    s3 = [vm(set_dims(o[2:]) + (32, w), F32) for o, w in orders]
    r3 = [vm((3, 32, w), F32) for o, w in orders]
    dma = pltpu.SemaphoreType.DMA
    scratch = (
        [vm(flat, BF)]
        + [vm((2, 4, 4, 2, 32, W), BF), vm((2, T, T), F32), vm((2, T, T), F32)]
        + [vm((2,) + state, F32), vm(state, F32)]
        + [vm(paired, BF)] * 4
        + [vm(state, BF), vm((2,) + state, BF), vm((2,) + state, BF)]
        + [vm(flat, F32), vm(flat, F32), vm(flat, BF), vm((W, 2 * T), BF), vm((W, 2 * T), BF)]
        + [vm((2 * T, HALF), BF), vm(flat, BF)]
        + [vm((2, 4, 4, 2, 32, HALF), BF)]
        + r1 + s2 + r2 + s3 + r3
        + [vm((32, HALF), F32)]
        + [dma((5,)), dma((5,)), dma((5,)), dma((27,)), dma((27,)), dma((12,)), dma((12,))]
        + [dma((32,)), dma((32,)), dma((32,)), dma((32,)), dma((27,)), dma((27,))]
    )
    smem = pl.BlockSpec(memory_space=pltpu.SMEM)
    outs = pl.pallas_call(
        kernel,
        name="linear_attention",
        out_shape=[pltpu.VMEM(flat, BF)] * 4 + [pltpu.VMEM((16, W), F32)],
        in_specs=[smem, smem, in_vmem] + [any_space] * 5,
        out_specs=[in_vmem] * 5,
        scratch_shapes=scratch,
        compiler_params=pltpu.CompilerParams(
            collective_id=0, has_side_effects=True, vmem_limit_bytes=52 * 1024 * 1024
        ),
    )(
        start_block, start_offset, norm_gain,
        query_rows.reshape(flat), key_rows.reshape(flat), value_rows.reshape(flat), out_grad.reshape(flat),
        out_weight,
    )
    shape = query_rows.shape
    return tuple(o.reshape(shape) for o in outs[:4]) + (outs[4],)


def solution(mesh):
    rows = P("dp", "ctx", None)
    spread = P(("dp", "ctx"), None)
    return jax.shard_map(
        per_device,
        mesh=mesh,
        in_specs=(rows, rows, rows, rows, P(), spread, P("dp", None), P("dp", None)),
        out_specs=(rows, rows, rows, rows, spread),
        check_vma=False,
    )
```

time: 146 us -> 104 us (0.71)
  Pallas kernels: 136 us -> 97.6 us
  local copies, waits for them, and re-layouts: 9.98 us -> 5.93 us
    pallas_call x1, Pallas kernels: 136 us -> 97.6 us  [per_device(): pl.pallas_call(kernel, name='linear_attention', out_shape=[pltpu.VMEM(fla...]
    unnamed x13 -> x5, local copies, waits for them, and re-layouts: 9.98 us -> 5.93 us
where the time goes in v2:
time: 104 us
  Pallas kernels  97.6 us (94%)
  local copies, waits for them, and re-layouts  5.93 us (6%)
    pallas_call x1, Pallas kernels, per_device(): pl.pallas_call(kernel, name='linear_attention', out_shape=[pltpu.VMEM(fla...  97.6 us
    unnamed x5, local copies, waits for them, and re-layouts  5.93 us

profile of v2, /device:TPU:1, one launch (start us, length us, event | category | flops | bytes accessed | tf_op | source)
XLA Modules:
  0.0 104.2 jit_solution(7677223761064972068)
XLA Ops:
  0.6 97.6 %linear_attention.1 = (bf16[512,2048]{1,0:T(8,128)(2,1)S(1)}, bf16[512,2048]{1,0:T(8,128)(2,1)S(1)}, bf16[512,2048]{1,0:T(8,128)(2,1)S(1)}, bf16[512,2048]{1,0:T(8,128)(2,1)S(1)}, f32[16,2048]{1,0:T(8,128)S(1)}) custom-call(s32[2,3]{1,0:T(2,128)} %sb.1, s32[2,3]{1,0:T(2,128)} %so.1, f32[16,128]{1,0:T(8,128)} %gain.1, bf16[512,2048]{1,0:T(8,128)(2,1)} %bitcast.12, ...), custom_call_target="tpu_custom_call" | custom-call | tf_op jit(solution)/shard_map/linear_attention/pallas_call | solution.py:544
  98.2 1.3 %copy.18 = bf16[2,256,2048]{2,1,0:T(8,128)(2,1)} copy(bf16[2,256,2048]{2,1,0:T(8,128)(2,1)S(1)} %bitcast.11) | data formatting | bytes 4194304
  99.5 1.3 %copy.19 = bf16[2,256,2048]{2,1,0:T(8,128)(2,1)} copy(bf16[2,256,2048]{2,1,0:T(8,128)(2,1)S(1)} %bitcast.10) | data formatting | bytes 4194304
  100.9 0.7 copy.22
  101.5 1.3 %copy.20 = bf16[2,256,2048]{2,1,0:T(8,128)(2,1)} copy(bf16[2,256,2048]{2,1,0:T(8,128)(2,1)S(1)} %bitcast.9) | data formatting | bytes 4194304
  102.8 1.3 %copy.21 = bf16[2,256,2048]{2,1,0:T(8,128)(2,1)} copy(bf16[2,256,2048]{2,1,0:T(8,128)(2,1)S(1)} %bitcast.8) | data formatting | bytes 4194304

commit v3 on v2

--- a/solution.py
+++ b/solution.py
@@ -43,13 +43,23 @@
     return (x, y, z, 1 - c)
 
 
-def chips(ref, at, held, free, cols=None, lead=()):
+def chips(ref, at, held, free, cols=None, half=None):
     x, y, z, _ = at
     every = slice(None)
-    parts = (("y", y % 2), ("z", z), ("x", x), ("y", y // 2))
-    index = tuple(every if axis in free else place for axis, place in parts if axis in held)
+    parts = (("y", y % 2, 2), ("z", z, 4), ("x", x, 4), ("y", y // 2, 2))
+    index = []
+    for axis, place, size in parts:
+        if axis not in held:
+            continue
+        if axis not in free:
+            index.append(place)
+        elif half is None:
+            index.append(every)
+        else:
+            index.append(pl.ds(half * size // 2, size // 2))
+            half = None
     tail = (every,) if cols is None else (every, cols)
-    return ref.at[tuple(lead) + index + tail]
+    return ref.at[tuple(index) + tail]
 
 
 def set_dims(held):
@@ -318,6 +328,42 @@
         dst = (r1, r2, r3)[phase][p].at[n - 1]
         return remote(src, dst, rss.at[i], rsr.at[i], to)
 
+    def first_step(p, kind, n, sending):
+        order = PIECES[p][2][::-1]
+        side = 0 if n == 1 else 1
+        half = 1 - side if kind == 1 else side
+        axis, free = order[0], order[1:]
+        whose = moved(me, axis, 2 if kind == 0 else n)
+        src = chips(part, whose, "xyz", free, pl.ds(PIECES[p][0], PIECES[p][1]), half)
+        size = set_dims(free)[0] // 2
+        dst = r1[p].at[1 if kind == 0 else n - 1, pl.ds(half * size, size)]
+        i = 27 + (kind * 2 + side) * 3 + p
+        to = moved(me, axis, n if sending else -n)
+        return remote(src, dst, rss.at[i], rsr.at[i], to)
+
+    def combine(p):
+        order = PIECES[p][2][::-1]
+        free = order[1:]
+        dims = set_dims(free)
+        dims = (dims[0] // 2,) + dims[1:]
+        for n in (1, 3):
+            first_step(p, 0, n, False).wait_recv()
+            half = 0 if n == 1 else 1
+            own = chips(part, moved(me, order[0], n), "xyz", free, pl.ds(PIECES[p][0], PIECES[p][1]), half)
+            got = r1[p].at[1, pl.ds(half * dims[0], dims[0])]
+
+            def one(i, _):
+                lead, rest = [], i
+                for d in dims[::-1]:
+                    lead = [rest % d] + lead
+                    rest = rest // d
+                lead = tuple(lead)
+                own[lead] = (own[lead].astype(F32) + got[lead].astype(F32)).astype(BF)
+                return 0
+
+            lax.fori_loop(0, math.prod(dims), one, 0)
+            first_step(p, 2, n, True).start()
+
     def product(p):
         first, width, _ = PIECES[p]
 
@@ -332,8 +378,9 @@
             return 0
 
         lax.fori_loop(0, 4, one, 0)
-        for n in (1, 2, 3):
-            spread(0, p, n, True).start()
+        for kind in (0, 1):
+            for n in (1, 3):
+                first_step(p, kind, n, True).start()
 
     def project(n, _):
         cols = pl.ds(pl.multiple_of(n * 256, 256), 256)
@@ -343,8 +390,14 @@
     def add_up(phase, p):
         order = PIECES[p][2][::-1]
         width = PIECES[p][1]
-        for n in (1, 2, 3):
-            spread(phase, p, n, False).wait_recv()
+        if phase == 0:
+            for n in (1, 3):
+                first_step(p, 1, n, False).wait_recv()
+                first_step(p, 2, n, False).wait_recv()
+        else:
+            for n in (1, 2, 3):
+                spread(phase, p, n, False).wait_recv()
+        terms = (0, 2) if phase == 0 else (0, 1, 2)
         free = order[phase + 1:]
         if phase == 0:
             own = chips(part, me, "xyz", free, pl.ds(PIECES[p][0], width))
@@ -354,7 +407,7 @@
         dims = set_dims(free)
         if phase == 2:
             total = own[...].astype(F32)
-            for n in range(3):
+            for n in terms:
                 total += got[n].astype(F32)
             rows[:, PIECES[p][0]:PIECES[p][0] + width] = total * (1.0 / 256.0)
             return
@@ -367,7 +420,7 @@
                 rest = rest // d
             lead = tuple(lead)
             total = own[lead].astype(F32)
-            for n in range(3):
+            for n in terms:
                 total += got[(n,) + lead].astype(F32)
             target[lead] = total.astype(target.dtype)
             return 0
@@ -412,11 +465,11 @@
             gather(2, p, n, False).wait_recv()
             forward(p, n, True).start()
 
-    pl.semaphore_wait(barrier, len(partners))
-    w_cross.start()
     loads[0].wait()
     loads[1].wait()
     over(0, 8, 2, kv)
+    pl.semaphore_wait(barrier, len(partners))
+    w_cross.start()
     ahead[0].begin()
     w_local.wait()
     w_cross.wait_recv()
@@ -469,8 +522,11 @@
             forward(p, n, False).wait_recv()
     lax.fori_loop(0, 4, gradient, 0)
     behind[0].begin()
+    combine(0)
+    combine(1)
     lax.fori_loop(4, 8, gradient, 0)
     behind[1].begin()
+    combine(2)
     behind[0].exchange()
     lax.fori_loop(0, 2, project, 0)
     behind[1].exchange()
@@ -507,7 +563,11 @@
         for phase in range(3):
             for n in (1, 2, 3):
                 gather(phase, p, n, True).wait_send()
-                spread(phase, p, n, True).wait_send()
+                if phase:
+                    spread(phase, p, n, True).wait_send()
+        for n in (1, 3):
+            for kind in range(3):
+                first_step(p, kind, n, True).wait_send()
     for scan in behind:
         scan.drain()
 
@@ -538,7 +598,7 @@
         + r1 + s2 + r2 + s3 + r3
         + [vm((32, HALF), F32)]
         + [dma((5,)), dma((5,)), dma((5,)), dma((27,)), dma((27,)), dma((12,)), dma((12,))]
-        + [dma((32,)), dma((32,)), dma((32,)), dma((32,)), dma((27,)), dma((27,))]
+        + [dma((32,)), dma((32,)), dma((32,)), dma((32,)), dma((45,)), dma((45,))]
     )
     smem = pl.BlockSpec(memory_space=pltpu.SMEM)
     outs = pl.pallas_call(

time: 104 us -> 108 us (1.038)
  the two profiles are of different devices: /device:TPU:1 before, /device:TPU:8 now
where the time goes in v3:
time: 108 us
  Pallas kernels  101 us (94%)
  local copies, waits for them, and re-layouts  5.93 us (5%)
    pallas_call x1, Pallas kernels, per_device(): pl.pallas_call(kernel, name='linear_attention', out_shape=[pltpu.VMEM(fla...  101 us
    unnamed x5, local copies, waits for them, and re-layouts  5.93 us

profile of v3, /device:TPU:8, one launch (start us, length us, event | category | flops | bytes accessed | tf_op | source)
XLA Modules:
  0.0 107.7 jit_solution(9130309018335700219)
XLA Ops:
  0.6 101.1 %linear_attention.1 = (bf16[512,2048]{1,0:T(8,128)(2,1)S(1)}, bf16[512,2048]{1,0:T(8,128)(2,1)S(1)}, bf16[512,2048]{1,0:T(8,128)(2,1)S(1)}, bf16[512,2048]{1,0:T(8,128)(2,1)S(1)}, f32[16,2048]{1,0:T(8,128)S(1)}) custom-call(s32[2,3]{1,0:T(2,128)} %sb.1, s32[2,3]{1,0:T(2,128)} %so.1, f32[16,128]{1,0:T(8,128)} %gain.1, bf16[512,2048]{1,0:T(8,128)(2,1)} %bitcast.12, ...), custom_call_target="tpu_custom_call" | custom-call | tf_op jit(solution)/shard_map/linear_attention/pallas_call | solution.py:604
  101.8 1.3 %copy.18 = bf16[2,256,2048]{2,1,0:T(8,128)(2,1)} copy(bf16[2,256,2048]{2,1,0:T(8,128)(2,1)S(1)} %bitcast.11) | data formatting | bytes 4194304
  103.1 1.3 %copy.19 = bf16[2,256,2048]{2,1,0:T(8,128)(2,1)} copy(bf16[2,256,2048]{2,1,0:T(8,128)(2,1)S(1)} %bitcast.10) | data formatting | bytes 4194304
  104.4 0.7 copy.22
  105.1 1.3 %copy.20 = bf16[2,256,2048]{2,1,0:T(8,128)(2,1)} copy(bf16[2,256,2048]{2,1,0:T(8,128)(2,1)S(1)} %bitcast.9) | data formatting | bytes 4194304
  106.4 1.3 %copy.21 = bf16[2,256,2048]{2,1,0:T(8,128)(2,1)} copy(bf16[2,256,2048]{2,1,0:T(8,128)(2,1)S(1)} %bitcast.8) | data formatting | bytes 4194304
